TPU v7x, 1024 devices: a whole 4x4x32 slice. The times are simulated.
1024 devices in a mesh: row: 8 (over y, x_lo), col: 128 (over x_hi, z, core).
Axes of the slice: x: 4 (x_hi: 2, x_lo: 2; x = x_hi * 2 + x_lo), y: 4, z: 32, core: 2. Of those that a mesh axis runs over, the one named last changes fastest.
Arguments:
- inputs: bfloat16 [1536, 1024], P(None, 'row'), may hold values from -6 to 6
- out_grad: bfloat16 [1536, 1024], P(None, 'row'), may hold values from -1.5 to 1.5
- w_in: bfloat16 [1024, 65536], P('row', 'col'), may hold values from -0.25 to 0.25
- w_out: bfloat16 [65536, 1024], P('col', 'row'), may hold values from -0.1875 to 0.1875
- in_keep: int32 [8, 512], P('row', 'col'), may hold values from 0 to 1, as said below
- out_keep: int32 [512, 8], P('col', 'row'), may hold values from 0 to 1, as said below
Outputs:
- w_in_grad: float32 [1024, 65536], P('row', 'col')
- w_out_grad: float32 [65536, 1024], P('col', 'row')
- in_grad: float32 [1536, 1024], P('col', 'row')
Inputs may be any that keep to these rules, and one draw needn't show every extreme that they name: `in_keep`: 1 where the 128 x 128 block of w_in is kept, 0 where it is pruned. `out_keep`: 1 where the 128 x 128 block of w_out is kept, 0 where it is pruned.
All inputs are finite; a program needn't handle non-finite values.
Results may differ from a plain program's by a relative error of at most 0.018.
Values may be sent and summed in bfloat16 or wider, within the bound.
A program may use at most 32 MiB of HBM per device.

v0:
```python
import jax
import jax.numpy as jnp
from jax import lax
from jax.sharding import PartitionSpec as P

BLOCK = 128


sqrt_two_pi = 0.7978845608028654
cubic_term = 0.044715


def prune_blocks(weight, keep):
    rows, cols = weight.shape
    blocks = weight.reshape(rows // BLOCK, BLOCK, cols // BLOCK, BLOCK)
    kept = jnp.where(keep[:, None, :, None] > 0, blocks, jnp.zeros_like(blocks))
    return kept.reshape(rows, cols)


def gelu_parts(value):
    tangent = jnp.tanh(sqrt_two_pi * (value + cubic_term * value * value * value))
    activated = 0.5 * value * (1.0 + tangent)
    gradient = 0.5 * (1.0 + tangent) + 0.5 * value * (1.0 - tangent * tangent) * sqrt_two_pi * (
        1.0 + 3.0 * cubic_term * value * value
    )
    return (activated, gradient)


def hidden_local(pre_act, act_grad):
    activated, gradient = gelu_parts(pre_act)
    return (activated.astype(jnp.bfloat16), (act_grad * gradient).astype(jnp.bfloat16))


def per_device(inputs, out_grad, w_in, w_out, in_keep, out_keep):
    kept_in = prune_blocks(w_in, in_keep)
    kept_out = prune_blocks(w_out, out_keep)
    pre_part = jnp.dot(inputs, kept_in, preferred_element_type=jnp.float32)
    grad_part = lax.dot_general(
        out_grad, kept_out, (((1,), (1,)), ((), ())), preferred_element_type=jnp.float32
    )
    pre_act, act_grad = (
        lax.psum_scatter(
            pre_part.astype(jnp.bfloat16), "row", scatter_dimension=0, tiled=True
        ).astype(jnp.float32),
        lax.psum_scatter(
            grad_part.astype(jnp.bfloat16), "row", scatter_dimension=0, tiled=True
        ).astype(jnp.float32),
    )
    activated, pre_grad = hidden_local(pre_act, act_grad)
    all_activated, all_pre_grad = (
        lax.all_gather(activated, "row", axis=0, tiled=True),
        lax.all_gather(pre_grad, "row", axis=0, tiled=True),
    )
    w_in_grad = lax.dot_general(
        inputs, all_pre_grad, (((0,), (0,)), ((), ())), preferred_element_type=jnp.float32
    )
    w_out_grad = lax.dot_general(
        all_activated, out_grad, (((0,), (0,)), ((), ())), preferred_element_type=jnp.float32
    )
    in_grad = lax.psum_scatter(
        lax.dot_general(
            all_pre_grad, kept_in, (((1,), (1,)), ((), ())), preferred_element_type=jnp.float32
        ),
        "col",
        scatter_dimension=0,
        tiled=True,
    )
    return (prune_blocks(w_in_grad, in_keep), prune_blocks(w_out_grad, out_keep), in_grad)


def solution(mesh):
    return jax.shard_map(
        per_device,
        mesh=mesh,
        in_specs=(
            P(None, "row"),
            P(None, "row"),
            P("row", "col"),
            P("col", "row"),
            P("row", "col"),
            P("col", "row"),
        ),
        out_specs=(P("row", "col"), P("col", "row"), P("col", "row")),
        check_vma=False,
    )
```

profile of v0, /device:TPU:1, one launch (start us, length us, event | category | flops | bytes accessed | tf_op | source)
XLA Modules:
  0.0 646.7 jit_solution(3253258732059080966)
XLA Ops:
  14.6 63.3 %reduce-scatter.11.cloned.1.call-done = bf16[192,512]{1,0:T(8,128)(2,1)} async-done(((bf16[1536,512]{1,0:T(8,128)(2,1)}), bf16[192,512]{1,0:T(8,128)(2,1)}) %reduce-scatter.11.cloned.1.call-update) | async-done | bytes 196624 | tf_op jit(solution)/shard_map/reduce_scatter | solution.py:42
  77.9 65.0 %reduce-scatter.9.cloned.1.call-done = bf16[192,512]{1,0:T(8,128)(2,1)} async-done(((bf16[1536,512]{1,0:T(8,128)(2,1)}), bf16[192,512]{1,0:T(8,128)(2,1)}) %reduce-scatter.9.cloned.1.call-update) | async-done | bytes 196624 | tf_op jit(solution)/shard_map/reduce_scatter | solution.py:45
  142.8 2.1 fusion.11
  145.5 62.2 %all-gather.3.cloned.1.call-done = bf16[1536,512]{1,0:T(8,128)(2,1)} async-done(((bf16[192,512]{1,0:T(8,128)(2,1)}), bf16[1536,512]{1,0:T(8,128)(2,1)}) %all-gather.3.cloned.1.call-update) | async-done | bytes 1572880 | tf_op jit(solution)/shard_map/all_gather | solution.py:52
  207.7 2.1 fusion.17
  209.8 264.8 %fusion = f32[16,128]{1,0:T(8,128)S(1)} fusion(f32[1536,128]{1,0:T(8,128)S(1)} %fusion.17), kind=kCustom, calls=%all-reduce-scatter | all-reduce-scatter fusion | flops 262145 | bytes 798720
  474.6 3.1 collective-permute-start
  481.6 13.9 %collective-permute-start.11 = (f32[16,128]{1,0:T(8,128)S(1)}, f32[16,128]{1,0:T(8,128)S(1)}, u32[]{:S(2)}, u32[]{:S(2)}) collective-permute-start(f32[16,128]{1,0:T(8,128)S(1)} %fusion), channel_id=1, source_target_pairs={{0,12},{1,13},{2,14},{3,15},{4,16},{5,17},{6,18},{7,19},{8,20},{9,... | collective-permute-start | bytes 24584
  495.5 7.5 %collective-permute-start.12 = (f32[16,128]{1,0:T(8,128)S(1)}, f32[16,128]{1,0:T(8,128)S(1)}, u32[]{:S(2)}, u32[]{:S(2)}) collective-permute-start(f32[16,128]{1,0:T(8,128)S(1)} %fusion), channel_id=1, source_target_pairs={{0,13},{1,14},{2,15},{3,16},{4,17},{5,18},{6,19},{7,20},{8,21},{9,... | collective-permute-start | bytes 24584
  503.0 7.1 %collective-permute-start.13 = (f32[16,128]{1,0:T(8,128)S(1)}, f32[16,128]{1,0:T(8,128)S(1)}, u32[]{:S(2)}, u32[]{:S(2)}) collective-permute-start(f32[16,128]{1,0:T(8,128)S(1)} %fusion), channel_id=1, source_target_pairs={{0,14},{1,15},{2,16},{3,17},{4,18},{5,19},{6,20},{7,21},{8,22},{9,... | collective-permute-start | bytes 24584
  510.1 7.4 %collective-permute-start.14 = (f32[16,128]{1,0:T(8,128)S(1)}, f32[16,128]{1,0:T(8,128)S(1)}, u32[]{:S(2)}, u32[]{:S(2)}) collective-permute-start(f32[16,128]{1,0:T(8,128)S(1)} %fusion), channel_id=1, source_target_pairs={{0,15},{1,16},{2,17},{3,18},{4,19},{5,20},{6,21},{7,22},{8,23},{9,... | collective-permute-start | bytes 24584
  517.6 2.5 collective-permute-start.15
  520.1 16.3 %collective-permute-start.16 = (f32[16,128]{1,0:T(8,128)S(1)}, f32[16,128]{1,0:T(8,128)S(1)}, u32[]{:S(2)}, u32[]{:S(2)}) collective-permute-start(f32[16,128]{1,0:T(8,128)S(1)} %fusion), channel_id=1, source_target_pairs={{0,17},{1,18},{2,19},{3,20},{4,21},{5,22},{6,23},{7,24},{8,25},{9,... | collective-permute-start | bytes 24584
  536.4 4.9 collective-permute-start.17
  541.4 2.2 collective-permute-start.18
  545.0 6.5 %collective-permute-start.2 = (f32[16,128]{1,0:T(8,128)S(1)}, f32[16,128]{1,0:T(8,128)S(1)}, u32[]{:S(2)}, u32[]{:S(2)}) collective-permute-start(f32[16,128]{1,0:T(8,128)S(1)} %fusion), channel_id=1, source_target_pairs={{0,3},{1,4},{2,5},{3,6},{4,7},{5,8},{6,9},{7,10},{8,11},{9,12},{10... | collective-permute-start | bytes 24584
  551.5 12.5 %collective-permute-start.20 = (f32[16,128]{1,0:T(8,128)S(1)}, f32[16,128]{1,0:T(8,128)S(1)}, u32[]{:S(2)}, u32[]{:S(2)}) collective-permute-start(f32[16,128]{1,0:T(8,128)S(1)} %fusion), channel_id=1, source_target_pairs={{0,21},{1,22},{2,23},{3,24},{4,25},{5,26},{6,27},{7,28},{8,29},{9,... | collective-permute-start | bytes 24584
  564.0 2.0 collective-permute-start.21
  566.0 3.5 collective-permute-start.22
  569.5 6.8 %collective-permute-start.23 = (f32[16,128]{1,0:T(8,128)S(1)}, f32[16,128]{1,0:T(8,128)S(1)}, u32[]{:S(2)}, u32[]{:S(2)}) collective-permute-start(f32[16,128]{1,0:T(8,128)S(1)} %fusion), channel_id=1, source_target_pairs={{0,24},{1,25},{2,26},{3,27},{4,28},{5,29},{6,30},{7,31},{8,32},{9,... | collective-permute-start | bytes 24584
  576.3 2.9 collective-permute-start.24
  581.1 3.4 collective-permute-start.26
  584.5 7.4 %collective-permute-start.27 = (f32[16,128]{1,0:T(8,128)S(1)}, f32[16,128]{1,0:T(8,128)S(1)}, u32[]{:S(2)}, u32[]{:S(2)}) collective-permute-start(f32[16,128]{1,0:T(8,128)S(1)} %fusion), channel_id=1, source_target_pairs={{0,28},{1,29},{2,30},{3,31},{4,32},{5,33},{6,34},{7,35},{8,36},{9,... | collective-permute-start | bytes 24584
  593.9 4.4 collective-permute-start.28
  599.8 5.7 collective-permute-start.3
  605.5 2.5 collective-permute-start.30
  611.9 5.5 collective-permute-start.6
  617.4 3.8 collective-permute-start.7
  621.2 3.8 collective-permute-start.8
  625.0 7.3 %collective-permute-start.9 = (f32[16,128]{1,0:T(8,128)S(1)}, f32[16,128]{1,0:T(8,128)S(1)}, u32[]{:S(2)}, u32[]{:S(2)}) collective-permute-start(f32[16,128]{1,0:T(8,128)S(1)} %fusion), channel_id=1, source_target_pairs={{0,10},{1,11},{2,12},{3,13},{4,14},{5,15},{6,16},{7,17},{8,18},{9,... | collective-permute-start | bytes 24584
  632.4 2.7 convolution_select_fusion
  635.9 3.6 concatenate
  (74 shorter events, 23.2 us)
Async XLA Ops:
  7.2 70.7 %reduce-scatter.11.cloned.1.call-start = ((), (), s32[]{:S(2)}) async-start(), calls=%async_computation.5 | async-start | bytes 1769472 | tf_op jit(solution)/shard_map/reduce_scatter | solution.py:42
  11.3 131.5 %reduce-scatter.9.cloned.1.call-start = ((), (), s32[]{:S(2)}) async-start(), calls=%async_computation.4 | async-start | bytes 1769472 | tf_op jit(solution)/shard_map/reduce_scatter | solution.py:45
  14.6 193.2 %all-gather.3.cloned.1.call-start = ((), (), s32[]{:S(2)}) async-start(), calls=%async_computation.2 | async-start | bytes 1769472 | tf_op jit(solution)/shard_map/all_gather | solution.py:52
  144.9 487.4 %all-gather.5.cloned.1.call-start = ((), (), s32[]{:S(2)}) async-start(), calls=%async_computation.3 | async-start | bytes 1769472 | tf_op jit(solution)/shard_map/all_gather | solution.py:51
  474.6 28.4 %collective-permute-start = (f32[16,128]{1,0:T(8,128)S(1)}, f32[16,128]{1,0:T(8,128)S(1)}, u32[]{:S(2)}, u32[]{:S(2)}) collective-permute-start(f32[16,128]{1,0:T(8,128)S(1)} %fusion), channel_id=1, source_target_pairs={{0,1},{1,2},{2,3},{3,4},{4,5},{5,6},{6,7},{7,8},{8,9},{9,10},{10,1... | collective-permute-start | bytes 24584
  477.7 17.8 %collective-permute-start.31 = (f32[12,128]{1,0:T(8,128)S(1)}, f32[12,128]{1,0:T(8,128)S(1)}, u32[]{:S(2)}, u32[]{:S(2)}) collective-permute-start(f32[12,128]{1,0:T(8,128)S(1)} %slice), channel_id=1, source_target_pairs={{0,32},{1,33},{2,34},{3,35},{4,36},{5,37},{6,38},{7,39},{8,40},{9,... | collective-permute-start | bytes 18440
  479.0 31.1 %collective-permute-start.1 = (f32[16,128]{1,0:T(8,128)S(1)}, f32[16,128]{1,0:T(8,128)S(1)}, u32[]{:S(2)}, u32[]{:S(2)}) collective-permute-start(f32[16,128]{1,0:T(8,128)S(1)} %fusion), channel_id=1, source_target_pairs={{0,2},{1,3},{2,4},{3,5},{4,6},{5,7},{6,8},{7,9},{8,10},{9,11},{10,... | collective-permute-start | bytes 24584
  480.3 37.3 %collective-permute-start.10 = (f32[16,128]{1,0:T(8,128)S(1)}, f32[16,128]{1,0:T(8,128)S(1)}, u32[]{:S(2)}, u32[]{:S(2)}) collective-permute-start(f32[16,128]{1,0:T(8,128)S(1)} %fusion), channel_id=1, source_target_pairs={{0,11},{1,12},{2,13},{3,14},{4,15},{5,16},{6,17},{7,18},{8,19},{9,... | collective-permute-start | bytes 24584
  481.6 38.6 %collective-permute-start.11 = (f32[16,128]{1,0:T(8,128)S(1)}, f32[16,128]{1,0:T(8,128)S(1)}, u32[]{:S(2)}, u32[]{:S(2)}) collective-permute-start(f32[16,128]{1,0:T(8,128)S(1)} %fusion), channel_id=1, source_target_pairs={{0,12},{1,13},{2,14},{3,15},{4,16},{5,17},{6,18},{7,19},{8,20},{9,... | collective-permute-start | bytes 24584
  495.5 40.9 %collective-permute-start.12 = (f32[16,128]{1,0:T(8,128)S(1)}, f32[16,128]{1,0:T(8,128)S(1)}, u32[]{:S(2)}, u32[]{:S(2)}) collective-permute-start(f32[16,128]{1,0:T(8,128)S(1)} %fusion), channel_id=1, source_target_pairs={{0,13},{1,14},{2,15},{3,16},{4,17},{5,18},{6,19},{7,20},{8,21},{9,... | collective-permute-start | bytes 24584
  503.0 38.3 %collective-permute-start.13 = (f32[16,128]{1,0:T(8,128)S(1)}, f32[16,128]{1,0:T(8,128)S(1)}, u32[]{:S(2)}, u32[]{:S(2)}) collective-permute-start(f32[16,128]{1,0:T(8,128)S(1)} %fusion), channel_id=1, source_target_pairs={{0,14},{1,15},{2,16},{3,17},{4,18},{5,19},{6,20},{7,21},{8,22},{9,... | collective-permute-start | bytes 24584
  510.1 33.5 %collective-permute-start.14 = (f32[16,128]{1,0:T(8,128)S(1)}, f32[16,128]{1,0:T(8,128)S(1)}, u32[]{:S(2)}, u32[]{:S(2)}) collective-permute-start(f32[16,128]{1,0:T(8,128)S(1)} %fusion), channel_id=1, source_target_pairs={{0,15},{1,16},{2,17},{3,18},{4,19},{5,20},{6,21},{7,22},{8,23},{9,... | collective-permute-start | bytes 24584
  517.6 27.4 %collective-permute-start.15 = (f32[16,128]{1,0:T(8,128)S(1)}, f32[16,128]{1,0:T(8,128)S(1)}, u32[]{:S(2)}, u32[]{:S(2)}) collective-permute-start(f32[16,128]{1,0:T(8,128)S(1)} %fusion), channel_id=1, source_target_pairs={{0,16},{1,17},{2,18},{3,19},{4,20},{5,21},{6,22},{7,23},{8,24},{9,... | collective-permute-start | bytes 24584
  520.1 31.3 %collective-permute-start.16 = (f32[16,128]{1,0:T(8,128)S(1)}, f32[16,128]{1,0:T(8,128)S(1)}, u32[]{:S(2)}, u32[]{:S(2)}) collective-permute-start(f32[16,128]{1,0:T(8,128)S(1)} %fusion), channel_id=1, source_target_pairs={{0,17},{1,18},{2,19},{3,20},{4,21},{5,22},{6,23},{7,24},{8,25},{9,... | collective-permute-start | bytes 24584
  536.4 27.6 %collective-permute-start.17 = (f32[16,128]{1,0:T(8,128)S(1)}, f32[16,128]{1,0:T(8,128)S(1)}, u32[]{:S(2)}, u32[]{:S(2)}) collective-permute-start(f32[16,128]{1,0:T(8,128)S(1)} %fusion), channel_id=1, source_target_pairs={{0,18},{1,19},{2,20},{3,21},{4,22},{5,23},{6,24},{7,25},{8,26},{9,... | collective-permute-start | bytes 24584
  541.4 24.6 %collective-permute-start.18 = (f32[16,128]{1,0:T(8,128)S(1)}, f32[16,128]{1,0:T(8,128)S(1)}, u32[]{:S(2)}, u32[]{:S(2)}) collective-permute-start(f32[16,128]{1,0:T(8,128)S(1)} %fusion), channel_id=1, source_target_pairs={{0,19},{1,20},{2,21},{3,22},{4,23},{5,24},{6,25},{7,26},{8,27},{9,... | collective-permute-start | bytes 24584
  543.6 25.9 %collective-permute-start.19 = (f32[16,128]{1,0:T(8,128)S(1)}, f32[16,128]{1,0:T(8,128)S(1)}, u32[]{:S(2)}, u32[]{:S(2)}) collective-permute-start(f32[16,128]{1,0:T(8,128)S(1)} %fusion), channel_id=1, source_target_pairs={{0,20},{1,21},{2,22},{3,23},{4,24},{5,25},{6,26},{7,27},{8,28},{9,... | collective-permute-start | bytes 24584
  545.0 31.3 %collective-permute-start.2 = (f32[16,128]{1,0:T(8,128)S(1)}, f32[16,128]{1,0:T(8,128)S(1)}, u32[]{:S(2)}, u32[]{:S(2)}) collective-permute-start(f32[16,128]{1,0:T(8,128)S(1)} %fusion), channel_id=1, source_target_pairs={{0,3},{1,4},{2,5},{3,6},{4,7},{5,8},{6,9},{7,10},{8,11},{9,12},{10... | collective-permute-start | bytes 24584
  551.5 27.7 %collective-permute-start.20 = (f32[16,128]{1,0:T(8,128)S(1)}, f32[16,128]{1,0:T(8,128)S(1)}, u32[]{:S(2)}, u32[]{:S(2)}) collective-permute-start(f32[16,128]{1,0:T(8,128)S(1)} %fusion), channel_id=1, source_target_pairs={{0,21},{1,22},{2,23},{3,24},{4,25},{5,26},{6,27},{7,28},{8,29},{9,... | collective-permute-start | bytes 24584
  564.0 17.0 %collective-permute-start.21 = (f32[16,128]{1,0:T(8,128)S(1)}, f32[16,128]{1,0:T(8,128)S(1)}, u32[]{:S(2)}, u32[]{:S(2)}) collective-permute-start(f32[16,128]{1,0:T(8,128)S(1)} %fusion), channel_id=1, source_target_pairs={{0,22},{1,23},{2,24},{3,25},{4,26},{5,27},{6,28},{7,29},{8,30},{9,... | collective-permute-start | bytes 24584
  566.0 18.5 %collective-permute-start.22 = (f32[16,128]{1,0:T(8,128)S(1)}, f32[16,128]{1,0:T(8,128)S(1)}, u32[]{:S(2)}, u32[]{:S(2)}) collective-permute-start(f32[16,128]{1,0:T(8,128)S(1)} %fusion), channel_id=1, source_target_pairs={{0,23},{1,24},{2,25},{3,26},{4,27},{5,28},{6,29},{7,30},{8,31},{9,... | collective-permute-start | bytes 24584
  569.5 24.3 %collective-permute-start.23 = (f32[16,128]{1,0:T(8,128)S(1)}, f32[16,128]{1,0:T(8,128)S(1)}, u32[]{:S(2)}, u32[]{:S(2)}) collective-permute-start(f32[16,128]{1,0:T(8,128)S(1)} %fusion), channel_id=1, source_target_pairs={{0,24},{1,25},{2,26},{3,27},{4,28},{5,29},{6,30},{7,31},{8,32},{9,... | collective-permute-start | bytes 24584
  576.3 22.0 %collective-permute-start.24 = (f32[16,128]{1,0:T(8,128)S(1)}, f32[16,128]{1,0:T(8,128)S(1)}, u32[]{:S(2)}, u32[]{:S(2)}) collective-permute-start(f32[16,128]{1,0:T(8,128)S(1)} %fusion), channel_id=1, source_target_pairs={{0,25},{1,26},{2,27},{3,28},{4,29},{5,30},{6,31},{7,32},{8,33},{9,... | collective-permute-start | bytes 24584
  579.2 20.6 %collective-permute-start.25 = (f32[16,128]{1,0:T(8,128)S(1)}, f32[16,128]{1,0:T(8,128)S(1)}, u32[]{:S(2)}, u32[]{:S(2)}) collective-permute-start(f32[16,128]{1,0:T(8,128)S(1)} %fusion), channel_id=1, source_target_pairs={{0,26},{1,27},{2,28},{3,29},{4,30},{5,31},{6,32},{7,33},{8,34},{9,... | collective-permute-start | bytes 24584
  581.1 24.5 %collective-permute-start.26 = (f32[16,128]{1,0:T(8,128)S(1)}, f32[16,128]{1,0:T(8,128)S(1)}, u32[]{:S(2)}, u32[]{:S(2)}) collective-permute-start(f32[16,128]{1,0:T(8,128)S(1)} %fusion), channel_id=1, source_target_pairs={{0,27},{1,28},{2,29},{3,30},{4,31},{5,32},{6,33},{7,34},{8,35},{9,... | collective-permute-start | bytes 24584
  584.5 23.5 %collective-permute-start.27 = (f32[16,128]{1,0:T(8,128)S(1)}, f32[16,128]{1,0:T(8,128)S(1)}, u32[]{:S(2)}, u32[]{:S(2)}) collective-permute-start(f32[16,128]{1,0:T(8,128)S(1)} %fusion), channel_id=1, source_target_pairs={{0,28},{1,29},{2,30},{3,31},{4,32},{5,33},{6,34},{7,35},{8,36},{9,... | collective-permute-start | bytes 24584
  593.9 16.1 %collective-permute-start.28 = (f32[16,128]{1,0:T(8,128)S(1)}, f32[16,128]{1,0:T(8,128)S(1)}, u32[]{:S(2)}, u32[]{:S(2)}) collective-permute-start(f32[16,128]{1,0:T(8,128)S(1)} %fusion), channel_id=1, source_target_pairs={{0,29},{1,30},{2,31},{3,32},{4,33},{5,34},{6,35},{7,36},{8,37},{9,... | collective-permute-start | bytes 24584
  599.8 17.6 %collective-permute-start.3 = (f32[16,128]{1,0:T(8,128)S(1)}, f32[16,128]{1,0:T(8,128)S(1)}, u32[]{:S(2)}, u32[]{:S(2)}) collective-permute-start(f32[16,128]{1,0:T(8,128)S(1)} %fusion), channel_id=1, source_target_pairs={{0,4},{1,5},{2,6},{3,7},{4,8},{5,9},{6,10},{7,11},{8,12},{9,13},{1... | collective-permute-start | bytes 24584
  608.0 17.0 %collective-permute-start.4 = (f32[16,128]{1,0:T(8,128)S(1)}, f32[16,128]{1,0:T(8,128)S(1)}, u32[]{:S(2)}, u32[]{:S(2)}) collective-permute-start(f32[16,128]{1,0:T(8,128)S(1)} %fusion), channel_id=1, source_target_pairs={{0,5},{1,6},{2,7},{3,8},{4,9},{5,10},{6,11},{7,12},{8,13},{9,14},{... | collective-permute-start | bytes 24584
  610.0 25.9 %collective-permute-start.5 = (f32[16,128]{1,0:T(8,128)S(1)}, f32[16,128]{1,0:T(8,128)S(1)}, u32[]{:S(2)}, u32[]{:S(2)}) collective-permute-start(f32[16,128]{1,0:T(8,128)S(1)} %fusion), channel_id=1, source_target_pairs={{0,6},{1,7},{2,8},{3,9},{4,10},{5,11},{6,12},{7,13},{8,14},{9,15},... | collective-permute-start | bytes 24584
  611.9 24.0 %collective-permute-start.6 = (f32[16,128]{1,0:T(8,128)S(1)}, f32[16,128]{1,0:T(8,128)S(1)}, u32[]{:S(2)}, u32[]{:S(2)}) collective-permute-start(f32[16,128]{1,0:T(8,128)S(1)} %fusion), channel_id=1, source_target_pairs={{0,7},{1,8},{2,9},{3,10},{4,11},{5,12},{6,13},{7,14},{8,15},{9,16}... | collective-permute-start | bytes 24584
  617.4 18.5 %collective-permute-start.7 = (f32[16,128]{1,0:T(8,128)S(1)}, f32[16,128]{1,0:T(8,128)S(1)}, u32[]{:S(2)}, u32[]{:S(2)}) collective-permute-start(f32[16,128]{1,0:T(8,128)S(1)} %fusion), channel_id=1, source_target_pairs={{0,8},{1,9},{2,10},{3,11},{4,12},{5,13},{6,14},{7,15},{8,16},{9,17... | collective-permute-start | bytes 24584
  (10 other events, 653.4 us)
Sparse Core Ops, SparseCore 0:
  11.4 66.3 reduce-scatter.10
  81.3 61.5 reduce-scatter.8
  146.1 61.5 all-gather.2
  210.8 62.1 all-gather.4
where the time goes:
time: 648 us; the launch traced here: 647 us
  blocking collectives  265 us (41%)
  waiting for transfers between devices  191 us (29%)
  starting transfers between devices  155 us (24%)
  between operations  15 us (2%)
  local copies, waits for them, and re-layouts  10.7 us (2%)
  matrix products  7.55 us (1%)
    unnamed x1, blocking collectives  265 us
    unnamed x32, starting transfers between devices  155 us
    reduce_scatter x1, waiting for transfers between devices, per_device(): lax.psum_scatter(grad_part.astype(jnp.bfloat16), 'row', scatter_dimension...  65 us
    reduce_scatter x1, waiting for transfers between devices, per_device(): lax.psum_scatter(pre_part.astype(jnp.bfloat16), 'row', scatter_dimension=...  63.3 us
    all_gather x1, waiting for transfers between devices, per_device(): lax.all_gather(pre_grad, 'row', axis=0, tiled=True)  62.2 us
  transfers between devices with their start and end apart: 36, of which 3 were waited for; matrix products, arithmetic and copies ran while one was open for 42% of the time, Pallas kernels for 0%

commit v1 on v0

v1 whole, which is shorter than its diff:
```python
import jax
import jax.numpy as jnp
from jax import lax
from jax.experimental import pallas as pl
from jax.experimental.pallas import tpu as pltpu
from jax.sharding import PartitionSpec as P

MESH = pl.DeviceIdType.MESH
BLOCK = 128
BF = jnp.bfloat16
F32 = jnp.float32

sqrt_two_pi = 0.7978845608028654
cubic_term = 0.044715

N_Y, N_XL, N_XH, N_Z = 4, 2, 2, 32
TOK = 384
HALF = 192
HID = 256
ROWS = 12


def gelu_parts(value):
    square = value * value
    tangent = jnp.tanh(sqrt_two_pi * value * (1.0 + cubic_term * square))
    upper = 0.5 * (1.0 + tangent)
    gradient = upper + 0.5 * value * (1.0 - tangent * tangent) * sqrt_two_pi * (
        1.0 + 3.0 * cubic_term * square
    )
    return value * upper, gradient


def nn(a, b):
    return jnp.dot(a, b, preferred_element_type=F32)


def nt(a, b):
    return lax.dot_general(a, b, (((1,), (1,)), ((), ())), preferred_element_type=F32)


class Names:
    def __init__(self):
        self.of = {}

    def __call__(self, *name):
        return self.of.setdefault(name, len(self.of))


N_SEM = 96


def kernel(
    inputs, out_grad, w_in, w_out, in_keep, out_keep,
    o_in, o_out, o_x,
    acts, win, wout, win_l, wout_l, win_s, wout_s, kin, kout, acts_t, pre, ag,
    v_in, v_out, ya_in, yb_out, y1_in, y1_out, y3_in, y3_out, s_in, s_out, x_in, x_out,
    q_b, q_r, q_s, z_r, f_s, f_r,
    send_sem, recv_sem, local_sem, relay_sem,
):
    row, col = lax.axis_index("row"), lax.axis_index("col")
    y, xl = row // N_XL, row % N_XL
    xh, z, k = col // (2 * N_Z), (col // 2) % N_Z, col % 2
    x = 2 * xh + xl
    h = z % 2
    pair = z + 1 - 2 * h

    def dev(y=y, x=x, z=z, k=k):
        return (y * N_XL + x % 2, ((x // 2) * N_Z + z) * 2 + k)

    def up(d):
        return (y + d) % N_Y

    def xr(d):
        return (x + d) % 4

    def along_z(d):
        return dev(z=(z + d + N_Z) % N_Z)

    core = dev(k=1 - k)
    inner = dev(x=2 * xh + 1 - xl)
    ydev = {d: dev(y=up(d)) for d in (1, 2, 3)}
    xdev = {d: dev(x=xr(d)) for d in (1, 3)}
    near = {
        (e, f): dev(x=xr(e), z=pair if f else z) for f in (0, 1) for e in range(4) if e or f
    }

    def owner(j):
        return dev(
            y=2 * (1 - xh) + k, x=2 * (y // 2) + xl, z=16 * (y % 2) + 8 * h + j // 2, k=j % 2
        )

    barrier = pltpu.get_barrier_semaphore()
    partners = [core, *ydev.values(), *near.values(), along_z(2 * h - 1)]
    partners += [dev(y=2 * xh + i, x=2 * (1 - y // 2) + xl, k=y % 2) for i in (0, 1)]
    for device in partners:
        pl.semaphore_signal(barrier, inc=1, device_id=device, device_id_type=MESH)

    names = Names()
    sent = []

    def copy(src, dst, name, device):
        i = names(*name)
        return pltpu.make_async_remote_copy(
            src_ref=src, dst_ref=dst, send_sem=send_sem.at[i], recv_sem=recv_sem.at[i],
            device_id=device, device_id_type=MESH,
        )

    def send(src, dst, name, device):
        c = copy(src, dst, name, device)
        c.start()
        sent.append(c)

    def arrived(dst, name):
        copy(dst, dst, name, core).wait_recv()

    def tell(r):
        for d in (-(1, 1, 2, 4, 8)[r], (1, 1, 2, 4, 8)[r]):
            pl.semaphore_signal(
                relay_sem.at[r], inc=1, device_id=along_z(d), device_id_type=MESH
            )

    def heard(r):
        pl.semaphore_wait(relay_sem.at[r], 2)

    local = [
        pltpu.make_async_copy(src, dst, local_sem.at[i])
        for i, (src, dst) in enumerate(
            ((w_in, win_l), (w_out, wout_l), (in_keep, kin), (out_keep, kout))
        )
    ]
    for c in local:
        c.start()
    for c in local:
        c.wait()

    def pruned_in(j):
        at = pl.ds(pl.multiple_of(j * BLOCK, BLOCK), BLOCK)
        return (win_l[:, at].astype(F32) * kin[0, j].astype(F32)).astype(BF)

    def pruned_out(j):
        at = pl.ds(pl.multiple_of(j * BLOCK, BLOCK), BLOCK)
        return (wout_l[at, :].astype(F32) * kout[0, j].astype(F32)).astype(BF)

    for jj in range(2):
        part = pl.ds(BLOCK * jj, BLOCK)
        win_s[:, part] = pruned_in(2 * (1 - xl) + jj)
        wout_s[part, :] = pruned_out(2 * (1 - xl) + jj)
        win[0, 0:BLOCK, part] = pruned_in(2 * xl + jj)
        wout[0, part, 0:BLOCK] = pruned_out(2 * xl + jj)

    pl.semaphore_wait(barrier, len(partners))

    mine = pl.ds(pl.multiple_of(HALF * xh, HALF), HALF)
    other = pl.ds(pl.multiple_of(HALF * (1 - xh), HALF), HALF)

    def tokens(of_y):
        return pl.ds(pl.multiple_of(TOK * of_y + HALF * xh, HALF), HALF)

    lo, hi = pl.ds(0, BLOCK), pl.ds(BLOCK, BLOCK)

    def win_at(d, p):
        return win.at[d, pl.ds(BLOCK * p, BLOCK), :]

    def wout_at(d, p):
        return wout.at[d, :, pl.ds(BLOCK * p, BLOCK)]

    def own_tokens(array):
        at = pl.ds(pl.multiple_of(TOK * y, TOK), TOK)
        return pltpu.make_async_copy(array.at[at, :], acts.at[k, 0, :, lo], local_sem.at[4])

    def first_copies(array):
        along_y = [
            copy(array.at[tokens(up(d)), :], acts.at[k, 4 - d, mine, lo], ("ay", 4 - d), ydev[d])
            for d in (1, 3, 2)
        ]
        along_x = [
            copy(array.at[tokens(y), :], acts.at[k, 0, mine, hi], ("ax", 0, 4 - d), xdev[d])
            for d in (1, 3)
        ]
        return along_y + along_x

    send(win_s, win_at(0, 1), ("wx_in",), inner)
    send(wout_s, wout_at(0, 1), ("wx_out",), inner)

    for i, array in enumerate((inputs, out_grad)):

        @pl.when(k == i)
        def _():
            for c in first_copies(array):
                c.start()
            own_tokens(array).start()

    sent += first_copies(inputs)

    def spread(p):
        for d in (1, 3):
            send(win_at(0, p), win_at(4 - d, p), ("wy_in", 4 - d, p), ydev[d])
            send(wout_at(0, p), wout_at(4 - d, p), ("wy_out", 4 - d, p), ydev[d])

    spread(0)
    tell(0)

    def pass_on(p):
        arrived(win_at(3, p), ("wy_in", 3, p))
        send(win_at(3, p), win_at(2, p), ("wf_in", p), ydev[1])
        arrived(wout_at(1, p), ("wy_out", 1, p))
        send(wout_at(1, p), wout_at(2, p), ("wf_out", p), ydev[3])

    def token_half(e):
        return pl.ds(pl.multiple_of(HALF * (xr(e) // 2), HALF), HALF)

    def from_x(d, e):
        return acts.at[k, d, token_half(e), hi]

    def both_x(d):
        for e in (1, 3):
            arrived(from_x(d, e), ("ax", d, e))
        if d == 2:
            away = 1 + 2 * k
            half = pl.ds(pl.multiple_of(HALF * (((x + 4 - away) % 4) // 2), HALF), HALF)
            send(
                acts.at[k, d, half, hi], acts.at[k, d, half, lo], ("af", d), dev(x=(x + away) % 4)
            )
        elif d:
            send(from_x(d, d), acts.at[k, d, token_half(d), lo], ("af", d), xdev[4 - d])

    def to_core(d):
        if d:
            arrived(acts.at[k, d, other, lo], ("af", d))
        send(acts.at[k, d], acts.at[k, d], ("ac", d), core)

    def products(d):
        for p in (0, 1):
            if d == 1:
                arrived(win_at(1, p), ("wy_in", 1, p))
            if d == 3:
                arrived(wout_at(3, p), ("wy_out", 3, p))
            if d == 2:
                arrived(win_at(2, p), ("wf_in", p))
                arrived(wout_at(2, p), ("wf_out", p))
        arrived(acts.at[1 - k, d], ("ac", d))
        a, b = nn(acts[0, d], win[d]), nt(acts[1, d], wout[d])
        if d == 0:
            pre[...], ag[...] = a, b
        else:
            pre[...] += a
            ag[...] += b

    for d in (3, 1, 2):
        here = acts.at[k, d, mine, lo]
        arrived(here, ("ay", d))
        for e in (1, 3):
            send(here, acts.at[k, d, mine, hi], ("ax", d, 4 - e), xdev[e])
        if d == 3:
            heard(0)
            tell(1)

    arrived(win_at(0, 1), ("wx_in",))
    arrived(wout_at(0, 1), ("wx_out",))
    spread(1)
    heard(1)
    tell(2)
    pass_on(0)
    own_tokens(inputs).wait()
    both_x(0)
    to_core(0)
    both_x(3)
    heard(2)
    tell(3)
    both_x(1)
    pass_on(1)
    both_x(2)
    to_core(3)
    products(0)
    to_core(1)
    products(3)
    to_core(2)
    heard(3)
    tell(4)
    products(1)
    products(2)

    activated, gradient = gelu_parts(pre[...])
    pg = (ag[...] * gradient).astype(BF)
    act_t = activated.astype(BF).T

    def slices(s, i):
        of_y = s + 2 * i
        q = nt(pg, win[(of_y - y + N_Y) % N_Y]).astype(BF)
        q_b[s, 2 * (1 - i) + xl] = q[:, 0:BLOCK]
        q_b[s, 2 * (1 - i) + 1 - xl] = q[:, BLOCK:]

    for i in (0, 1):
        slices(1 - k, i)
        half = pl.ds(2 * (1 - i), 2)
        send(q_b.at[1 - k, half], q_r.at[half], ("q", i), core)
    for i in (0, 1):
        slices(k, i)

    def rows_of(f):
        return pl.ds(pl.multiple_of(HALF * ((h + f) % 2), HALF), HALF)

    for i in (0, 1):
        half = pl.ds(2 * (1 - i), 2)
        arrived(q_r.at[half], ("q", i))
        q_s[half] = (q_b[k, half].astype(F32) + q_r[half].astype(F32)).astype(BF)

    for e, f in ((2, 1), (1, 1), (3, 1), (2, 0), (1, 0), (3, 0), (0, 1)):
        send(
            q_s.at[xr(e), rows_of(f)], z_r.at[4 * f + (4 - e) % 4], ("z", (4 - e) % 4, f), near[e, f]
        )
    total = q_s[x, rows_of(0)].astype(F32)
    for e, f in ((1, 0), (3, 0), (0, 1), (1, 1), (3, 1), (2, 0), (2, 1)):
        arrived(z_r.at[4 * f + e], ("z", e, f))
        total += z_r[4 * f + e].astype(F32)

    f_s[...] = jnp.zeros_like(f_s)
    for j in range(16):
        f_s[j, 0:ROWS] = total[ROWS * j : ROWS * (j + 1)].astype(BF)
    heard(4)
    group = z // 2
    first = [names("f", g) for g in range(16)][0]
    for j in range(16):
        c = pltpu.make_async_remote_copy(
            src_ref=f_s.at[j], dst_ref=f_r.at[group], send_sem=send_sem.at[first + j],
            recv_sem=recv_sem.at[first + group], device_id=owner(j), device_id_type=MESH,
        )
        c.start()
        sent.append(c)

    def grads(d):
        acts_t[...] = acts[0, d].T
        v_in[d] = nn(acts_t[...], pg).astype(BF)
        v_out[d] = nn(act_t, acts[1, d]).astype(BF)

    grads(2)
    send(v_in.at[2], ya_in, ("ya",), ydev[1])
    send(v_out.at[2], yb_out, ("yb",), ydev[3])
    grads(1)
    send(v_out.at[1], y1_out, ("y1_out",), ydev[1])
    grads(3)
    send(v_in.at[3], y3_in, ("y3_in",), ydev[3])
    grads(0)

    arrived(ya_in, ("ya",))
    v_in[1] = (v_in[1].astype(F32) + ya_in[...].astype(F32)).astype(BF)
    send(v_in.at[1], y1_in, ("y1_in",), ydev[1])
    arrived(yb_out, ("yb",))
    v_out[3] = (v_out[3].astype(F32) + yb_out[...].astype(F32)).astype(BF)
    send(v_out.at[3], y3_out, ("y3_out",), ydev[3])

    arrived(y1_in, ("y1_in",))
    arrived(y3_in, ("y3_in",))
    s_in[...] = v_in[0].astype(F32) + y1_in[...].astype(F32) + y3_in[...].astype(F32)
    x_in[0] = s_in[BLOCK:].astype(BF)
    send(x_in.at[0], x_in.at[1], ("gx_in",), inner)
    arrived(y1_out, ("y1_out",))
    arrived(y3_out, ("y3_out",))
    s_out[...] = v_out[0].astype(F32) + y1_out[...].astype(F32) + y3_out[...].astype(F32)
    x_out[0] = s_out[:, BLOCK:].astype(BF)
    send(x_out.at[0], x_out.at[1], ("gx_out",), inner)

    def store_in(j, value):
        at = pl.ds(pl.multiple_of(j * BLOCK, BLOCK), BLOCK)
        o_in[:, at] = value * kin[0, j].astype(F32)

    def store_out(j, value):
        at = pl.ds(pl.multiple_of(j * BLOCK, BLOCK), BLOCK)
        o_out[at, :] = value * kout[0, j].astype(F32)

    cuts = [pl.ds(BLOCK * jj, BLOCK) for jj in (0, 1)]
    for jj, cut in enumerate(cuts):
        store_in(2 * xl + jj, s_in[0:BLOCK, cut])
        store_out(2 * xl + jj, s_out[cut, 0:BLOCK])
    arrived(x_in.at[1], ("gx_in",))
    for jj, cut in enumerate(cuts):
        store_in(2 * (1 - xl) + jj, x_in[1, :, cut].astype(F32))
    arrived(x_out.at[1], ("gx_out",))
    for jj, cut in enumerate(cuts):
        store_out(2 * (1 - xl) + jj, x_out[1, cut, :].astype(F32))

    for c in sent:
        c.wait_send()

    for g in range(16):
        arrived(f_r.at[g], ("f", g))
    last = f_r[0].astype(F32)
    for g in range(1, 16):
        last += f_r[g].astype(F32)
    o_x[...] = last[0:ROWS]


def per_device(inputs, out_grad, w_in, w_out, in_keep, out_keep):
    arrays = [
        pltpu.with_memory_space_constraint(array, pltpu.HBM)
        for array in (inputs, out_grad, w_in, w_out, in_keep, out_keep.reshape(1, -1))
    ]
    vmem = pl.BlockSpec(memory_space=pltpu.VMEM)
    hbm = pl.BlockSpec(memory_space=pltpu.HBM)
    B, H, V = BLOCK, HID, pltpu.VMEM
    return pl.pallas_call(
        kernel,
        out_shape=(
            jax.ShapeDtypeStruct((B, 2 * H), F32),
            jax.ShapeDtypeStruct((2 * H, B), F32),
            jax.ShapeDtypeStruct((ROWS, B), F32),
        ),
        in_specs=[hbm] * 6,
        out_specs=[vmem, vmem, vmem],
        scratch_shapes=[
            V((2, 4, TOK, 2 * B), BF),
            V((4, 2 * B, H), BF),
            V((4, H, 2 * B), BF),
            V((B, 2 * H), BF),
            V((2 * H, B), BF),
            V((B, H), BF),
            V((H, B), BF),
            pltpu.SMEM((1, 4), jnp.int32),
            pltpu.SMEM((1, 4), jnp.int32),
            V((2 * B, TOK), BF),
            V((TOK, H), F32),
            V((TOK, H), F32),
            V((4, 2 * B, H), BF),
            V((4, H, 2 * B), BF),
            V((2 * B, H), BF),
            V((H, 2 * B), BF),
            V((2 * B, H), BF),
            V((H, 2 * B), BF),
            V((2 * B, H), BF),
            V((H, 2 * B), BF),
            V((2 * B, H), F32),
            V((H, 2 * B), F32),
            V((2, B, H), BF),
            V((2, H, B), BF),
            V((2, 4, TOK, B), BF),
            V((4, TOK, B), BF),
            V((4, TOK, B), BF),
            V((8, HALF, B), BF),
            V((16, 16, B), BF),
            V((16, 16, B), BF),
            pltpu.SemaphoreType.DMA((N_SEM,)),
            pltpu.SemaphoreType.DMA((N_SEM,)),
            pltpu.SemaphoreType.DMA((5,)),
            pltpu.SemaphoreType.REGULAR((5,)),
        ],
        compiler_params=pltpu.CompilerParams(
            collective_id=0, has_side_effects=True, vmem_limit_bytes=48 * 1024 * 1024
        ),
    )(*arrays)


def solution(mesh):
    return jax.shard_map(
        per_device,
        mesh=mesh,
        in_specs=(
            P(None, "row"),
            P(None, "row"),
            P("row", "col"),
            P("col", "row"),
            P("row", "col"),
            P("col", "row"),
        ),
        out_specs=(P("row", "col"), P("col", "row"), P("col", "row")),
        check_vma=False,
    )
```

time: 648 us -> 72.3 us (0.11)
  the two profiles are of different devices: /device:TPU:1 before, /device:TPU:39 now
where the time goes in v1:
time: 72.3 us; the launch traced here: 72.1 us
  Pallas kernels  69.5 us (96%)
  local copies, waits for them, and re-layouts  2.01 us (3%)
    pallas_call x1, Pallas kernels, per_device(): pl.pallas_call(kernel, out_shape=(jax.ShapeDtypeStruct((B, 2 * H), F32),...  69.5 us
    unnamed x3, local copies, waits for them, and re-layouts  2.01 us

profile of v1, /device:TPU:39, one launch (start us, length us, event | category | flops | bytes accessed | tf_op | source)
XLA Modules:
  0.0 72.1 jit_solution(9288857765789472831)
XLA Ops:
  0.6 69.5 %shard_map.85 = (f32[128,512]{1,0:T(8,128)S(1)}, f32[512,128]{1,0:T(8,128)S(1)}, f32[12,128]{1,0:T(8,128)S(1)}) custom-call(bf16[1536,128]{1,0:T(8,128)(2,1)} %inputs.1, bf16[1536,128]{1,0:T(8,128)(2,1)} %out_grad.1, bf16[128,512]{1,0:T(8,128)(2,1)} %w_in.1, bf16[512,128]{1,0:T(8,128)(2,1)} %w_out.1, s32[1,4]{1,0:T(1,128)} %in_keep.1, s32[1,4]{1,0:T(1,128)} %bitcast.1), custom_call_target="tpu_custom_call" | custom-call | tf_op jit(solution)/shard_map/pallas_call | solution.py:401
  70.1 0.7 copy.12
  70.8 0.7 copy.13
  71.5 0.6 copy.14

commit v2 on v1

--- a/solution.py
+++ b/solution.py
@@ -86,7 +86,10 @@
 
     def owner(j):
         return dev(
-            y=2 * (1 - xh) + k, x=2 * (y // 2) + xl, z=16 * (y % 2) + 8 * h + j // 2, k=j % 2
+            y=2 * (1 - xh) + k,
+            x=2 * (y // 2) + xl,
+            z=8 * (j // 4) + 4 * h + 2 * (y % 2) + j % 4 // 2,
+            k=j % 2,
         )
 
     barrier = pltpu.get_barrier_semaphore()
@@ -150,11 +153,13 @@
 
     pl.semaphore_wait(barrier, len(partners))
 
-    mine = pl.ds(pl.multiple_of(HALF * xh, HALF), HALF)
-    other = pl.ds(pl.multiple_of(HALF * (1 - xh), HALF), HALF)
-
-    def tokens(of_y):
-        return pl.ds(pl.multiple_of(TOK * of_y + HALF * xh, HALF), HALF)
+    def runs(half):
+        return pl.ds(4 * half, 4)
+
+    mine, other = runs(xh), runs(1 - xh)
+
+    def tokens(array, of_y, half):
+        return array.at[of_y // 2, :, half, of_y % 2]
 
     lo, hi = pl.ds(0, BLOCK), pl.ds(BLOCK, BLOCK)
 
@@ -165,16 +170,22 @@
         return wout.at[d, :, pl.ds(BLOCK * p, BLOCK)]
 
     def own_tokens(array):
-        at = pl.ds(pl.multiple_of(TOK * y, TOK), TOK)
-        return pltpu.make_async_copy(array.at[at, :], acts.at[k, 0, :, lo], local_sem.at[4])
+        return [
+            pltpu.make_async_copy(
+                tokens(array, y, half), acts.at[k, 0, runs(half), :, lo], local_sem.at[4 + half]
+            )
+            for half in (0, 1)
+        ]
 
     def first_copies(array):
         along_y = [
-            copy(array.at[tokens(up(d)), :], acts.at[k, 4 - d, mine, lo], ("ay", 4 - d), ydev[d])
+            copy(
+                tokens(array, up(d), xh), acts.at[k, 4 - d, mine, :, lo], ("ay", 4 - d), ydev[d]
+            )
             for d in (1, 3, 2)
         ]
         along_x = [
-            copy(array.at[tokens(y), :], acts.at[k, 0, mine, hi], ("ax", 0, 4 - d), xdev[d])
+            copy(tokens(array, y, xh), acts.at[k, 0, mine, :, hi], ("ax", 0, 4 - d), xdev[d])
             for d in (1, 3)
         ]
         return along_y + along_x
@@ -186,9 +197,8 @@
 
         @pl.when(k == i)
         def _():
-            for c in first_copies(array):
+            for c in first_copies(array) + own_tokens(array):
                 c.start()
-            own_tokens(array).start()
 
     sent += first_copies(inputs)
 
@@ -207,27 +217,33 @@
         send(wout_at(1, p), wout_at(2, p), ("wf_out", p), ydev[3])
 
     def token_half(e):
-        return pl.ds(pl.multiple_of(HALF * (xr(e) // 2), HALF), HALF)
+        return runs(xr(e) // 2)
 
     def from_x(d, e):
-        return acts.at[k, d, token_half(e), hi]
+        return acts.at[k, d, token_half(e), :, hi]
 
     def both_x(d):
         for e in (1, 3):
             arrived(from_x(d, e), ("ax", d, e))
         if d == 2:
             away = 1 + 2 * k
-            half = pl.ds(pl.multiple_of(HALF * (((x + 4 - away) % 4) // 2), HALF), HALF)
+            half = runs(((x + 4 - away) % 4) // 2)
             send(
-                acts.at[k, d, half, hi], acts.at[k, d, half, lo], ("af", d), dev(x=(x + away) % 4)
+                acts.at[k, d, half, :, hi],
+                acts.at[k, d, half, :, lo],
+                ("af", d),
+                dev(x=(x + away) % 4),
             )
         elif d:
-            send(from_x(d, d), acts.at[k, d, token_half(d), lo], ("af", d), xdev[4 - d])
+            send(from_x(d, d), acts.at[k, d, token_half(d), :, lo], ("af", d), xdev[4 - d])
 
     def to_core(d):
         if d:
-            arrived(acts.at[k, d, other, lo], ("af", d))
+            arrived(acts.at[k, d, other, :, lo], ("af", d))
         send(acts.at[k, d], acts.at[k, d], ("ac", d), core)
+
+    def flat(i, d):
+        return acts[i, d].reshape(TOK, 2 * BLOCK)
 
     def products(d):
         for p in (0, 1):
@@ -239,7 +255,7 @@
                 arrived(win_at(2, p), ("wf_in", p))
                 arrived(wout_at(2, p), ("wf_out", p))
         arrived(acts.at[1 - k, d], ("ac", d))
-        a, b = nn(acts[0, d], win[d]), nt(acts[1, d], wout[d])
+        a, b = nn(flat(0, d), win[d]), nt(flat(1, d), wout[d])
         if d == 0:
             pre[...], ag[...] = a, b
         else:
@@ -247,10 +263,10 @@
             ag[...] += b
 
     for d in (3, 1, 2):
-        here = acts.at[k, d, mine, lo]
+        here = acts.at[k, d, mine, :, lo]
         arrived(here, ("ay", d))
         for e in (1, 3):
-            send(here, acts.at[k, d, mine, hi], ("ax", d, 4 - e), xdev[e])
+            send(here, acts.at[k, d, mine, :, hi], ("ax", d, 4 - e), xdev[e])
         if d == 3:
             heard(0)
             tell(1)
@@ -261,7 +277,8 @@
     heard(1)
     tell(2)
     pass_on(0)
-    own_tokens(inputs).wait()
+    for c in own_tokens(inputs):
+        c.wait()
     both_x(0)
     to_core(0)
     both_x(3)
@@ -329,9 +346,9 @@
         sent.append(c)
 
     def grads(d):
-        acts_t[...] = acts[0, d].T
+        acts_t[...] = flat(0, d).T
         v_in[d] = nn(acts_t[...], pg).astype(BF)
-        v_out[d] = nn(act_t, acts[1, d]).astype(BF)
+        v_out[d] = nn(act_t, flat(1, d)).astype(BF)
 
     grads(2)
     send(v_in.at[2], ya_in, ("ya",), ydev[1])
@@ -390,15 +407,31 @@
     o_x[...] = last[0:ROWS]
 
 
+def write_out(a, b, c, a_out, b_out, c_out, sem):
+    pairs = ((a, a_out), (b, b_out), (c, c_out))
+    copies = [pltpu.make_async_copy(src, dst, sem.at[i]) for i, (src, dst) in enumerate(pairs)]
+    for one in copies:
+        one.start()
+    for one in copies:
+        one.wait()
+
+
 def per_device(inputs, out_grad, w_in, w_out, in_keep, out_keep):
     arrays = [
         pltpu.with_memory_space_constraint(array, pltpu.HBM)
-        for array in (inputs, out_grad, w_in, w_out, in_keep, out_keep.reshape(1, -1))
+        for array in (
+            inputs.reshape(2, 4, 2, 2, TOK // 8, BLOCK),
+            out_grad.reshape(2, 4, 2, 2, TOK // 8, BLOCK),
+            w_in,
+            w_out,
+            in_keep,
+            out_keep.reshape(1, -1),
+        )
     ]
     vmem = pl.BlockSpec(memory_space=pltpu.VMEM)
     hbm = pl.BlockSpec(memory_space=pltpu.HBM)
     B, H, V = BLOCK, HID, pltpu.VMEM
-    return pl.pallas_call(
+    results = pl.pallas_call(
         kernel,
         out_shape=(
             jax.ShapeDtypeStruct((B, 2 * H), F32),
@@ -408,7 +441,7 @@
         in_specs=[hbm] * 6,
         out_specs=[vmem, vmem, vmem],
         scratch_shapes=[
-            V((2, 4, TOK, 2 * B), BF),
+            V((2, 4, 8, TOK // 8, 2 * B), BF),
             V((4, 2 * B, H), BF),
             V((4, H, 2 * B), BF),
             V((B, 2 * H), BF),
@@ -440,13 +473,21 @@
             V((16, 16, B), BF),
             pltpu.SemaphoreType.DMA((N_SEM,)),
             pltpu.SemaphoreType.DMA((N_SEM,)),
-            pltpu.SemaphoreType.DMA((5,)),
+            pltpu.SemaphoreType.DMA((6,)),
             pltpu.SemaphoreType.REGULAR((5,)),
         ],
         compiler_params=pltpu.CompilerParams(
             collective_id=0, has_side_effects=True, vmem_limit_bytes=48 * 1024 * 1024
         ),
     )(*arrays)
+    return pl.pallas_call(
+        write_out,
+        out_shape=tuple(jax.ShapeDtypeStruct(r.shape, r.dtype) for r in results),
+        in_specs=[vmem] * 3,
+        out_specs=[hbm] * 3,
+        scratch_shapes=[pltpu.SemaphoreType.DMA((3,))],
+        compiler_params=pltpu.CompilerParams(vmem_limit_bytes=4 * 1024 * 1024),
+    )(*results)
 
 
 def solution(mesh):

time: 72.3 us -> 64.9 us (0.90)
  the two profiles are of different devices: /device:TPU:39 before, /device:TPU:1 now
where the time goes in v2:
time: 64.9 us; the launch traced here: 64 us
  Pallas kernels  63.3 us (98%)
    pallas_call x1, Pallas kernels, per_device(): pl.pallas_call(kernel, out_shape=(jax.ShapeDtypeStruct((B, 2 * H), F32),...  62.5 us

profile of v2, /device:TPU:1, one launch (start us, length us, event | category | flops | bytes accessed | tf_op | source)
XLA Modules:
  0.0 64.0 jit_solution(255451030353680479)
XLA Ops:
  0.6 62.5 %shard_map.85 = (f32[128,512]{1,0:T(8,128)S(1)}, f32[512,128]{1,0:T(8,128)S(1)}, f32[12,128]{1,0:T(8,128)S(1)}) custom-call(bf16[2,4,2,2,48,128]{5,4,3,2,1,0:T(8,128)(2,1)} %bitcast.3, bf16[2,4,2,2,48,128]{5,4,3,2,1,0:T(8,128)(2,1)} %bitcast.4, bf16[128,512]{1,0:T(8,128)(2,1)} %w_in.1, bf16[512,128]{1,0:T(8,128)(2,1)} %w_out.1, s32[1,4]{1,0:T(1,128)} %in_keep.1, ...), custom_call_target="tpu_custom_call" | custom-call | tf_op jit(solution)/shard_map/pallas_call | solution.py:434
  63.1 0.8 %shard_map.86 = (f32[128,512]{1,0:T(8,128)}, f32[512,128]{1,0:T(8,128)}, f32[12,128]{1,0:T(8,128)}) custom-call(f32[128,512]{1,0:T(8,128)S(1)} %get-tuple-element.6.a, f32[512,128]{1,0:T(8,128)S(1)} %get-tuple-element.7.b, f32[12,128]{1,0:T(8,128)S(1)} %get-tuple-element.8.c), custom_call_target="tpu_custom_call" | custom-call | tf_op jit(solution)/shard_map/pallas_call | solution.py:483

commit v3 on v2

--- a/solution.py
+++ b/solution.py
@@ -1,3 +1,5 @@
+import functools
+
 import jax
 import jax.numpy as jnp
 from jax import lax
@@ -20,14 +22,19 @@
 ROWS = 12
 
 
-def gelu_parts(value):
-    square = value * value
-    tangent = jnp.tanh(sqrt_two_pi * value * (1.0 + cubic_term * square))
-    upper = 0.5 * (1.0 + tangent)
-    gradient = upper + 0.5 * value * (1.0 - tangent * tangent) * sqrt_two_pi * (
-        1.0 + 3.0 * cubic_term * square
+def tangent_of(value):
+    return jnp.tanh(sqrt_two_pi * value * (1.0 + cubic_term * value * value))
+
+
+def gelu(value):
+    return 0.5 * value * (1.0 + tangent_of(value))
+
+
+def gelu_slope(value):
+    t = tangent_of(value)
+    return 0.5 * (1.0 + t) + 0.5 * value * (1.0 - t * t) * sqrt_two_pi * (
+        1.0 + 3.0 * cubic_term * value * value
     )
-    return value * upper, gradient
 
 
 def nn(a, b):
@@ -54,7 +61,7 @@
     o_in, o_out, o_x,
     acts, win, wout, win_l, wout_l, win_s, wout_s, kin, kout, acts_t, pre, ag,
     v_in, v_out, ya_in, yb_out, y1_in, y1_out, y3_in, y3_out, s_in, s_out, x_in, x_out,
-    q_b, q_r, q_s, z_r, f_s, f_r,
+    q_o, q_m, q_r, q_s, z_r, f_s, f_r,
     send_sem, recv_sem, local_sem, relay_sem,
 ):
     row, col = lax.axis_index("row"), lax.axis_index("col")
@@ -85,16 +92,11 @@
     }
 
     def owner(j):
-        return dev(
-            y=2 * (1 - xh) + k,
-            x=2 * (y // 2) + xl,
-            z=8 * (j // 4) + 4 * h + 2 * (y % 2) + j % 4 // 2,
-            k=j % 2,
-        )
+        return dev(y=up(2 * h + k), z=8 * (j // 4) + 2 * y + j % 4 // 2, k=j % 2)
 
     barrier = pltpu.get_barrier_semaphore()
     partners = [core, *ydev.values(), *near.values(), along_z(2 * h - 1)]
-    partners += [dev(y=2 * xh + i, x=2 * (1 - y // 2) + xl, k=y % 2) for i in (0, 1)]
+    partners += [dev(y=up(d), k=1 - k) for d in (1, 2, 3)]
     for device in partners:
         pl.semaphore_signal(barrier, inc=1, device_id=device, device_id_type=MESH)
 
@@ -159,7 +161,7 @@
     mine, other = runs(xh), runs(1 - xh)
 
     def tokens(array, of_y, half):
-        return array.at[of_y // 2, :, half, of_y % 2]
+        return array.at[half, :, of_y]
 
     lo, hi = pl.ds(0, BLOCK), pl.ds(BLOCK, BLOCK)
 
@@ -182,7 +184,7 @@
             copy(
                 tokens(array, up(d), xh), acts.at[k, 4 - d, mine, :, lo], ("ay", 4 - d), ydev[d]
             )
-            for d in (1, 3, 2)
+            for d in (2, 1, 3)
         ]
         along_x = [
             copy(tokens(array, y, xh), acts.at[k, 0, mine, :, hi], ("ax", 0, 4 - d), xdev[d])
@@ -297,37 +299,39 @@
     products(1)
     products(2)
 
-    activated, gradient = gelu_parts(pre[...])
-    pg = (ag[...] * gradient).astype(BF)
-    act_t = activated.astype(BF).T
-
-    def slices(s, i):
-        of_y = s + 2 * i
-        q = nt(pg, win[(of_y - y + N_Y) % N_Y]).astype(BF)
-        q_b[s, 2 * (1 - i) + xl] = q[:, 0:BLOCK]
-        q_b[s, 2 * (1 - i) + 1 - xl] = q[:, BLOCK:]
-
-    for i in (0, 1):
-        slices(1 - k, i)
-        half = pl.ds(2 * (1 - i), 2)
-        send(q_b.at[1 - k, half], q_r.at[half], ("q", i), core)
-    for i in (0, 1):
-        slices(k, i)
-
-    def rows_of(f):
-        return pl.ds(pl.multiple_of(HALF * ((h + f) % 2), HALF), HALF)
-
-    for i in (0, 1):
-        half = pl.ds(2 * (1 - i), 2)
-        arrived(q_r.at[half], ("q", i))
-        q_s[half] = (q_b[k, half].astype(F32) + q_r[half].astype(F32)).astype(BF)
-
-    for e, f in ((2, 1), (1, 1), (3, 1), (2, 0), (1, 0), (3, 0), (0, 1)):
-        send(
-            q_s.at[xr(e), rows_of(f)], z_r.at[4 * f + (4 - e) % 4], ("z", (4 - e) % 4, f), near[e, f]
-        )
-    total = q_s[x, rows_of(0)].astype(F32)
-    for e, f in ((1, 0), (3, 0), (0, 1), (1, 1), (3, 1), (2, 0), (2, 1)):
+    pg = (ag[...] * gelu_slope(pre[...])).astype(BF)
+
+    def slices(buffer, to_h, d):
+        q = nt(pg, win[d]).astype(BF)
+        buffer[to_h, 0] = q[:, 0:BLOCK]
+        buffer[to_h, 1] = q[:, BLOCK:]
+
+    def parity(f):
+        return (h + f) % 2
+
+    for f in (1, 0):
+        slices(q_o, parity(f), 2 * parity(f) + 1 - k)
+        send(q_o.at[parity(f)], q_r.at[parity(f)], ("q", f), core)
+    for f in (1, 0):
+        slices(q_m, parity(f), 2 * parity(f) + k)
+
+    def rows_of(e):
+        return pl.ds(pl.multiple_of(HALF * (xr(e) // 2), HALF), HALF)
+
+    for f in (1, 0):
+        to_h = parity(f)
+        arrived(q_r.at[to_h], ("q", f))
+        q_s[to_h] = (q_m[to_h].astype(F32) + q_r[to_h].astype(F32)).astype(BF)
+        for e in (2, 1, 3, 0):
+            if e or f:
+                send(
+                    q_s.at[to_h, e % 2, rows_of(e)],
+                    z_r.at[4 * f + (4 - e) % 4],
+                    ("z", (4 - e) % 4, f),
+                    near[e, f],
+                )
+    total = q_s[h, 0, rows_of(0)].astype(F32)
+    for e, f in ((0, 1), (1, 1), (3, 1), (1, 0), (3, 0), (2, 1), (2, 0)):
         arrived(z_r.at[4 * f + e], ("z", e, f))
         total += z_r[4 * f + e].astype(F32)
 
@@ -337,13 +341,30 @@
     heard(4)
     group = z // 2
     first = [names("f", g) for g in range(16)][0]
+    own_owner = (h == 0) & (k == 0) & (z % 8 == 2 * y)
+
+    def unless(own, act):
+        if own is None:
+            act()
+        else:
+            pl.when(jnp.logical_not(own))(act)
+
+    far = []
     for j in range(16):
+        own = own_owner & (z // 8 == j // 4) if j % 4 == 0 else None
         c = pltpu.make_async_remote_copy(
             src_ref=f_s.at[j], dst_ref=f_r.at[group], send_sem=send_sem.at[first + j],
             recv_sem=recv_sem.at[first + group], device_id=owner(j), device_id_type=MESH,
         )
-        c.start()
-        sent.append(c)
+        unless(own, c.start)
+        far.append((own, c.wait_send))
+        if own is not None:
+
+            @pl.when(own)
+            def _():
+                f_r[group] = f_s[j]
+
+    act_t = gelu(pre[...]).astype(BF).T
 
     def grads(d):
         acts_t[...] = flat(0, d).T
@@ -398,9 +419,11 @@
 
     for c in sent:
         c.wait_send()
+    for own, wait in far:
+        unless(own, wait)
 
     for g in range(16):
-        arrived(f_r.at[g], ("f", g))
+        unless(own_owner & (group == g), functools.partial(arrived, f_r.at[g], ("f", g)))
     last = f_r[0].astype(F32)
     for g in range(1, 16):
         last += f_r[g].astype(F32)
@@ -420,8 +443,8 @@
     arrays = [
         pltpu.with_memory_space_constraint(array, pltpu.HBM)
         for array in (
-            inputs.reshape(2, 4, 2, 2, TOK // 8, BLOCK),
-            out_grad.reshape(2, 4, 2, 2, TOK // 8, BLOCK),
+            inputs.reshape(2, 4, 4, TOK // 8, BLOCK),
+            out_grad.reshape(2, 4, 4, TOK // 8, BLOCK),
             w_in,
             w_out,
             in_keep,
@@ -465,9 +488,10 @@
             V((H, 2 * B), F32),
             V((2, B, H), BF),
             V((2, H, B), BF),
-            V((2, 4, TOK, B), BF),
-            V((4, TOK, B), BF),
-            V((4, TOK, B), BF),
+            V((2, 2, TOK, B), BF),
+            V((2, 2, TOK, B), BF),
+            V((2, 2, TOK, B), BF),
+            V((2, 2, TOK, B), BF),
             V((8, HALF, B), BF),
             V((16, 16, B), BF),
             V((16, 16, B), BF),

time: 64.9 us -> 62.4 us (0.961); the launches traced: 64 us -> 62.2 us
  Pallas kernels: 63.3 us -> 61.6 us
    pallas_call x1, Pallas kernels: 62.5 us -> 60.8 us  [per_device(): pl.pallas_call(kernel, out_shape=(jax.ShapeDtypeStruct((B, 2 * H), F32),...]
where the time goes in v3:
time: 62.4 us; the launch traced here: 62.2 us
  Pallas kernels  61.6 us (99%)
  between operations  0.64 us (1%)
    pallas_call x1, Pallas kernels, per_device(): pl.pallas_call(kernel, out_shape=(jax.ShapeDtypeStruct((B, 2 * H), F32),...  60.8 us

profile of v3, /device:TPU:1, one launch (start us, length us, event | category | flops | bytes accessed | tf_op | source)
XLA Modules:
  0.0 62.2 jit_solution(1705585400735293859)
XLA Ops:
  0.6 60.8 %shard_map.85 = (f32[128,512]{1,0:T(8,128)S(1)}, f32[512,128]{1,0:T(8,128)S(1)}, f32[12,128]{1,0:T(8,128)S(1)}) custom-call(bf16[2,4,4,48,128]{4,3,2,1,0:T(8,128)(2,1)} %bitcast.3, bf16[2,4,4,48,128]{4,3,2,1,0:T(8,128)(2,1)} %bitcast.4, bf16[128,512]{1,0:T(8,128)(2,1)} %w_in.1, bf16[512,128]{1,0:T(8,128)(2,1)} %w_out.1, s32[1,4]{1,0:T(1,128)} %in_keep.1, ...), custom_call_target="tpu_custom_call" | custom-call | tf_op jit(solution)/shard_map/pallas_call | solution.py:457
  61.4 0.8 %shard_map.86 = (f32[128,512]{1,0:T(8,128)}, f32[512,128]{1,0:T(8,128)}, f32[12,128]{1,0:T(8,128)}) custom-call(f32[128,512]{1,0:T(8,128)S(1)} %get-tuple-element.6.a, f32[512,128]{1,0:T(8,128)S(1)} %get-tuple-element.7.b, f32[12,128]{1,0:T(8,128)S(1)} %get-tuple-element.8.c), custom_call_target="tpu_custom_call" | custom-call | tf_op jit(solution)/shard_map/pallas_call | solution.py:507

commit v4 on v3

--- a/solution.py
+++ b/solution.py
@@ -135,24 +135,6 @@
     ]
     for c in local:
         c.start()
-    for c in local:
-        c.wait()
-
-    def pruned_in(j):
-        at = pl.ds(pl.multiple_of(j * BLOCK, BLOCK), BLOCK)
-        return (win_l[:, at].astype(F32) * kin[0, j].astype(F32)).astype(BF)
-
-    def pruned_out(j):
-        at = pl.ds(pl.multiple_of(j * BLOCK, BLOCK), BLOCK)
-        return (wout_l[at, :].astype(F32) * kout[0, j].astype(F32)).astype(BF)
-
-    for jj in range(2):
-        part = pl.ds(BLOCK * jj, BLOCK)
-        win_s[:, part] = pruned_in(2 * (1 - xl) + jj)
-        wout_s[part, :] = pruned_out(2 * (1 - xl) + jj)
-        win[0, 0:BLOCK, part] = pruned_in(2 * xl + jj)
-        wout[0, part, 0:BLOCK] = pruned_out(2 * xl + jj)
-
     pl.semaphore_wait(barrier, len(partners))
 
     def runs(half):
@@ -190,7 +172,32 @@
             copy(tokens(array, y, xh), acts.at[k, 0, mine, :, hi], ("ax", 0, 4 - d), xdev[d])
             for d in (1, 3)
         ]
-        return along_y + along_x
+        return along_y, along_x
+
+    for i, array in enumerate((inputs, out_grad)):
+
+        @pl.when(k == i)
+        def _():
+            for c in first_copies(array)[0] + own_tokens(array):
+                c.start()
+
+    for c in local:
+        c.wait()
+
+    def pruned_in(j):
+        at = pl.ds(pl.multiple_of(j * BLOCK, BLOCK), BLOCK)
+        return (win_l[:, at].astype(F32) * kin[0, j].astype(F32)).astype(BF)
+
+    def pruned_out(j):
+        at = pl.ds(pl.multiple_of(j * BLOCK, BLOCK), BLOCK)
+        return (wout_l[at, :].astype(F32) * kout[0, j].astype(F32)).astype(BF)
+
+    for jj in range(2):
+        part = pl.ds(BLOCK * jj, BLOCK)
+        win_s[:, part] = pruned_in(2 * (1 - xl) + jj)
+        wout_s[part, :] = pruned_out(2 * (1 - xl) + jj)
+        win[0, 0:BLOCK, part] = pruned_in(2 * xl + jj)
+        wout[0, part, 0:BLOCK] = pruned_out(2 * xl + jj)
 
     send(win_s, win_at(0, 1), ("wx_in",), inner)
     send(wout_s, wout_at(0, 1), ("wx_out",), inner)
@@ -199,10 +206,11 @@
 
         @pl.when(k == i)
         def _():
-            for c in first_copies(array) + own_tokens(array):
+            for c in first_copies(array)[1]:
                 c.start()
 
-    sent += first_copies(inputs)
+    for copies in first_copies(inputs):
+        sent += copies
 
     def spread(p):
         for d in (1, 3):

time: 62.4 us -> 62.3 us (level)
  no operation moved by 1% of the time
where the time goes in v4:
time: 62.3 us; the launch traced here: 62.2 us
  Pallas kernels  61.6 us (99%)
  between operations  0.64 us (1%)
    pallas_call x1, Pallas kernels, per_device(): pl.pallas_call(kernel, out_shape=(jax.ShapeDtypeStruct((B, 2 * H), F32),...  60.7 us

profile of v4, /device:TPU:1, one launch (start us, length us, event | category | flops | bytes accessed | tf_op | source)
XLA Modules:
  0.0 62.2 jit_solution(5474034641125480139)
XLA Ops:
  0.6 60.7 %shard_map.85 = (f32[128,512]{1,0:T(8,128)S(1)}, f32[512,128]{1,0:T(8,128)S(1)}, f32[12,128]{1,0:T(8,128)S(1)}) custom-call(bf16[2,4,4,48,128]{4,3,2,1,0:T(8,128)(2,1)} %bitcast.3, bf16[2,4,4,48,128]{4,3,2,1,0:T(8,128)(2,1)} %bitcast.4, bf16[128,512]{1,0:T(8,128)(2,1)} %w_in.1, bf16[512,128]{1,0:T(8,128)(2,1)} %w_out.1, s32[1,4]{1,0:T(1,128)} %in_keep.1, ...), custom_call_target="tpu_custom_call" | custom-call | tf_op jit(solution)/shard_map/pallas_call | solution.py:465
  61.4 0.8 %shard_map.86 = (f32[128,512]{1,0:T(8,128)}, f32[512,128]{1,0:T(8,128)}, f32[12,128]{1,0:T(8,128)}) custom-call(f32[128,512]{1,0:T(8,128)S(1)} %get-tuple-element.6.a, f32[512,128]{1,0:T(8,128)S(1)} %get-tuple-element.7.b, f32[12,128]{1,0:T(8,128)S(1)} %get-tuple-element.8.c), custom_call_target="tpu_custom_call" | custom-call | tf_op jit(solution)/shard_map/pallas_call | solution.py:515

commit v5 on v3

--- a/solution.py
+++ b/solution.py
@@ -288,12 +288,11 @@
     tell(3)
     both_x(1)
     pass_on(1)
+    products(0)
     both_x(2)
-    to_core(3)
-    products(0)
-    to_core(1)
+    for d in (3, 1, 2):
+        to_core(d)
     products(3)
-    to_core(2)
     heard(3)
     tell(4)
     products(1)

time: 62.4 us -> 62 us (level)
  Pallas kernels: 61.6 us -> 60.9 us
    pallas_call x1, Pallas kernels: 60.8 us -> 60.1 us  [per_device(): pl.pallas_call(kernel, out_shape=(jax.ShapeDtypeStruct((B, 2 * H), F32),...]
where the time goes in v5:
time: 62 us; the launch traced here: 61.6 us
  Pallas kernels  60.9 us (98%)
  between operations  0.64 us (1%)
    pallas_call x1, Pallas kernels, per_device(): pl.pallas_call(kernel, out_shape=(jax.ShapeDtypeStruct((B, 2 * H), F32),...  60.1 us

profile of v5, /device:TPU:1, one launch (start us, length us, event | category | flops | bytes accessed | tf_op | source)
XLA Modules:
  0.0 61.6 jit_solution(5622842701612338606)
XLA Ops:
  0.6 60.1 %shard_map.85 = (f32[128,512]{1,0:T(8,128)S(1)}, f32[512,128]{1,0:T(8,128)S(1)}, f32[12,128]{1,0:T(8,128)S(1)}) custom-call(bf16[2,4,4,48,128]{4,3,2,1,0:T(8,128)(2,1)} %bitcast.3, bf16[2,4,4,48,128]{4,3,2,1,0:T(8,128)(2,1)} %bitcast.4, bf16[128,512]{1,0:T(8,128)(2,1)} %w_in.1, bf16[512,128]{1,0:T(8,128)(2,1)} %w_out.1, s32[1,4]{1,0:T(1,128)} %in_keep.1, ...), custom_call_target="tpu_custom_call" | custom-call | tf_op jit(solution)/shard_map/pallas_call | solution.py:456
  60.8 0.8 %shard_map.86 = (f32[128,512]{1,0:T(8,128)}, f32[512,128]{1,0:T(8,128)}, f32[12,128]{1,0:T(8,128)}) custom-call(f32[128,512]{1,0:T(8,128)S(1)} %get-tuple-element.6.a, f32[512,128]{1,0:T(8,128)S(1)} %get-tuple-element.7.b, f32[12,128]{1,0:T(8,128)S(1)} %get-tuple-element.8.c), custom_call_target="tpu_custom_call" | custom-call | tf_op jit(solution)/shard_map/pallas_call | solution.py:506
